TPU v7x, 512 devices: a whole 4x4x16 slice. The times are simulated.
512 devices in a mesh: inst: 8 (over x_hi, y), space: 64 (over z, x_lo, core).
Axes of the slice: x: 4 (x_hi: 2, x_lo: 2; x = x_hi * 2 + x_lo), y: 4, z: 16, core: 2. Of those that a mesh axis runs over, the one named last changes fastest.
Arguments:
- adjoint_start: float32 [32, 5, 64, 8, 128], P('inst', None, 'space'), may hold values from -4 to 4
- objective_gradient: float32 [32, 5, 64, 8, 128], P('inst', None, 'space'), may hold values from -24 to 24
- diag_block: bfloat16 [32, 5, 5, 64, 8, 128], P('inst', None, None, 'space'), may hold values from -1.25 to 8
- precond_inverse: bfloat16 [32, 5, 5, 64, 8, 128], P('inst', None, None, 'space'), may hold values from -0.0625 to 0.165
- jac_span: bfloat16 [32, 5, 5, 64, 8, 128], P('inst', None, None, 'space'), may hold values from -3 to 3
- jac_normal: bfloat16 [32, 5, 5, 64, 8, 128], P('inst', None, None, 'space'), may hold values from -3 to 3
- jac_chord: bfloat16 [32, 5, 5, 64, 8, 128], P('inst', None, None, 'space'), may hold values from -3 to 3
- colour: int32 [64, 8, 128], P('space'), may hold values from 0 to 3
- wall_vector: float32 [32, 5, 64, 128], P('inst', None, 'space'), may hold values from -0.9 to 0.9
- section_owner: int32 [64, 128], P('space'), may hold values from 0 to 511
Outputs:
- adjoint_out: float32 [32, 5, 64, 8, 128], P('inst', None, 'space')
- section_sens: float32 [32, 512], P('inst', 'space')
All inputs are finite; a program needn't handle non-finite values.
Results may differ from a plain program's by a relative error of at most 0.0003.
Values sent between devices are 32-bit elements; how exact they have to be, the bound alone decides.
A program may use at most 64 MiB of HBM per device.

v0:
```python
import math

import jax
import jax.numpy as jnp
from jax import lax
from jax.sharding import PartitionSpec as P

NCOL = 4
SWEEPS = 2
PSTEPS = 2
SEC_DEV = 8


spectral_gain = 0.25


def with_halo(block, sides, width):
    for axis, dim in sides:
        count = lax.axis_size(axis)
        forward = [(i, i + 1) for i in range(count - 1)]
        backward = [(target, source) for source, target in forward]
        low = lax.ppermute(
            lax.slice_in_dim(block, block.shape[dim] - width, None, axis=dim), axis, forward
        )
        high = lax.ppermute(lax.slice_in_dim(block, 0, width, axis=dim), axis, backward)
        block = jnp.concatenate([low, block, high], axis=dim)
    return block


def spectral_table(instances_all):
    table_rows = []
    for row_index in range(instances_all):
        row_values = []
        for col_index in range(instances_all):
            offset_gap = col_index - row_index
            if offset_gap == 0:
                row_values.append(0.0)
            else:
                parity_sign = 1.0 if offset_gap % 2 == 0 else -1.0
                row_values.append(
                    spectral_gain
                    * 0.5
                    * parity_sign
                    / math.tan(math.pi * offset_gap / instances_all)
                )
        table_rows.append(row_values)
    return table_rows


def apply_block(blocks, values_in):
    return jnp.sum(blocks.astype(jnp.float32) * values_in[:, None], axis=2)


def coupling(jac_span, jac_normal, jac_chord, values_in, minus_span, plus_span):
    zeros_rim = jnp.zeros_like(values_in[:, :, :, :1])
    minus_normal = jnp.concatenate([zeros_rim, values_in[:, :, :, :-1]], axis=3)
    plus_normal = jnp.concatenate([values_in[:, :, :, 1:], zeros_rim], axis=3)
    minus_chord = jnp.roll(values_in, 1, axis=4)
    plus_chord = jnp.roll(values_in, -1, axis=4)
    running = apply_block(jac_span, minus_span - plus_span)
    running = running + apply_block(jac_normal, minus_normal - plus_normal)
    running = running + apply_block(jac_chord, minus_chord - plus_chord)
    return 0.5 * running


def on_device(
    adjoint_start,
    objective_gradient,
    diag_block,
    precond_inverse,
    jac_span,
    jac_normal,
    jac_chord,
    colour,
    wall_vector,
    section_owner,
):
    members = adjoint_start.shape[0]
    instances_all = members * lax.axis_size("inst")
    coefficients = jnp.asarray(spectral_table(instances_all), jnp.float32)
    adjoint = adjoint_start
    for pseudo_step in range(PSTEPS):
        padded = with_halo(adjoint, (("space", 2),), 1)
        local_part = apply_block(diag_block, adjoint) + coupling(
            jac_span, jac_normal, jac_chord, adjoint, padded[:, :, :-2], padded[:, :, 2:]
        )
        own_rows = lax.dynamic_slice_in_dim(
            coefficients, lax.axis_index("inst") * members, members, 0
        )
        spectral = jnp.einsum(
            "mn,nkxyz->mkxyz",
            own_rows,
            lax.all_gather(adjoint, "inst", axis=0, tiled=True),
            precision=lax.Precision.HIGHEST,
        )
        right_side = objective_gradient - (local_part + spectral)
        update = jnp.zeros_like(right_side)
        for sweep_index in range(SWEEPS):
            if sweep_index == 0:
                lower_rim = jnp.zeros_like(update)
                upper_rim = jnp.zeros_like(update)
            else:
                rimmed = with_halo(update, (("space", 2),), 1)
                lower_rim = rimmed[:, :, :1]
                upper_rim = rimmed[:, :, -1:]
            if sweep_index % 2 == 0:
                colour_order = list(range(NCOL))
            else:
                colour_order = list(range(NCOL - 1, -1, -1))
            for colour_value in colour_order:
                minus_span = jnp.concatenate([lower_rim, update[:, :, :-1]], axis=2)
                plus_span = jnp.concatenate([update[:, :, 1:], upper_rim], axis=2)
                updated = apply_block(
                    precond_inverse,
                    right_side
                    - coupling(jac_span, jac_normal, jac_chord, update, minus_span, plus_span),
                )
                update = jnp.where(colour == colour_value, updated, update)
        adjoint = adjoint + update
    wall_term = jnp.sum(wall_vector * adjoint[:, :, :, 0, :], axis=1)
    owners = section_owner.reshape(-1)
    sections_all = SEC_DEV * lax.axis_size("space")
    one_hot = (owners[:, None] == jnp.arange(sections_all, dtype=jnp.int32)[None, :]).astype(
        jnp.float32
    )
    partial_sums = jnp.dot(
        wall_term.reshape(members, -1),
        one_hot,
        precision=lax.Precision.HIGHEST,
        preferred_element_type=jnp.float32,
    )
    section_sens = lax.psum_scatter(partial_sums, "space", scatter_dimension=1, tiled=True)
    return (adjoint, section_sens)


def solution(mesh):
    return jax.shard_map(
        on_device,
        mesh=mesh,
        in_specs=(
            P("inst", None, "space", None, None),
            P("inst", None, "space", None, None),
            P("inst", None, None, "space", None, None),
            P("inst", None, None, "space", None, None),
            P("inst", None, None, "space", None, None),
            P("inst", None, None, "space", None, None),
            P("inst", None, None, "space", None, None),
            P("space", None, None),
            P("inst", None, "space", None),
            P("space", None),
        ),
        out_specs=(P("inst", None, "space", None, None), P("inst", "space")),
        check_vma=False,
    )
```

profile of v0, /device:TPU:256, one launch (start us, length us, event | category | flops | bytes accessed | tf_op | source)
XLA Modules:
  0.0 250.1 jit_solution(5463905200732190331)
XLA Ops:
  0.6 2.1 collective-permute-start
  2.7 5.8 %collective-permute-start.1 = (f32[4,5,1,8,128]{4,3,2,1,0:T(8,128)}, f32[4,5,1,8,128]{4,3,2,1,0:T(8,128)S(1)}, u32[]{:S(2)}, u32[]{:S(2)}) collective-permute-start(f32[4,5,1,8,128]{4,3,2,1,0:T(8,128)} %param.11), channel_id=1, source_target_pairs={{1,0},{2,1},{3,2},{4,3},{5,4},{6,5},{7,6},{8,7},{9,8},{10,9},{11,1... | collective-permute-start | bytes 245768 | tf_op jit(solution)/shard_map/ppermute | solution.py:25
  8.5 1.0 fusion.122
  9.6 36.2 %all_gather.6 = f32[32,5,1,8,128]{4,3,2,1,0:T(8,128)S(1)} all-gather(f32[4,5,1,8,128]{4,3,2,1,0:T(8,128)S(1)} %copy-done.3), channel_id=1, replica_groups=mesh['inst'=8,'space'=64] {'inst'}, dimensions={0}, use_global_device_ids=true | all-gather | bytes 737280 | tf_op jit(solution)/shard_map/all_gather | solution.py:93
  46.0 0.2 copy.366
  46.2 0.2 copy.367
  46.3 0.2 copy.368
  46.5 0.7 copy-done.9
  47.3 1.3 dynamic-slice
  49.2 1.2 fusion.2
  50.5 0.8 copy-done.1
  51.5 0.8 copy-done
  52.5 0.9 copy-done.4
  53.4 0.8 copy-done.6
  54.3 0.9 copy-done.2
  55.6 0.2 copy.373
  55.8 0.2 copy.374
  56.0 0.2 copy.375
  56.9 0.2 copy.377
  57.1 0.2 copy.378
  57.3 0.2 copy.379
  58.2 0.2 copy.381
  58.4 0.2 copy.382
  58.6 0.2 copy.383
  59.4 1.9 collective-permute-start.2
  61.3 5.8 %collective-permute-start.3 = (f32[4,5,1,8,128]{4,3,1,0,2:T(8,128)S(1)}, f32[4,5,1,8,128]{4,3,1,0,2:T(8,128)S(1)}, u32[]{:S(2)}, u32[]{:S(2)}) collective-permute-start(f32[4,5,1,8,128]{4,3,1,0,2:T(8,128)S(1)} %bitcast_select_fusion.12), channel_id=1, source_target_pairs={{1,0},{2,1},{3,2},{4,3},{5,4},{6,5},{7,6},{8,7},{9,8},{10,9},{11,1... | collective-permute-start | bytes 245768 | tf_op jit(solution)/shard_map/ppermute | solution.py:25
  67.2 0.2 copy.385
  67.4 0.2 copy.386
  67.6 0.2 copy.387
  68.1 1.0 collective-permute-done.3
  69.6 0.2 copy.389
  70.0 0.2 copy.391
  70.9 0.2 copy.393
  71.3 0.2 copy.395
  72.3 0.2 copy.397
  72.6 0.2 copy.399
  73.4 1.9 collective-permute-start.4
  75.3 5.8 %collective-permute-start.5 = (f32[4,5,1,8,128]{4,3,1,0,2:T(8,128)S(1)}, f32[4,5,1,8,128]{4,3,1,0,2:T(8,128)S(1)}, u32[]{:S(2)}, u32[]{:S(2)}) collective-permute-start(f32[4,5,1,8,128]{4,3,1,0,2:T(8,128)S(1)} %fusion.73), channel_id=1, source_target_pairs={{1,0},{2,1},{3,2},{4,3},{5,4},{6,5},{7,6},{8,7},{9,8},{10,9},{11,1... | collective-permute-start | bytes 245768 | tf_op jit(solution)/shard_map/ppermute | solution.py:25
  81.2 35.6 %all_gather.7 = f32[32,5,1,8,128]{4,3,2,1,0:T(8,128)S(1)} all-gather(f32[4,5,1,8,128]{4,3,2,1,0:T(8,128)S(1)} %bitcast.322), channel_id=1, replica_groups=mesh['inst'=8,'space'=64] {'inst'}, dimensions={0}, use_global_device_ids=true | all-gather | bytes 737280 | tf_op jit(solution)/shard_map/all_gather | solution.py:93
  116.8 1.2 fusion
  118.2 0.2 copy.402
  118.6 0.2 copy.404
  119.6 0.2 copy.410
  120.0 0.2 copy.412
  120.9 0.2 copy.414
  121.3 0.2 copy.416
  122.2 0.2 copy.418
  122.6 0.2 copy.420
  123.4 1.9 collective-permute-start.6
  125.3 5.8 %collective-permute-start.7 = (f32[4,5,1,8,128]{4,3,1,0,2:T(8,128)S(1)}, f32[4,5,1,8,128]{4,3,1,0,2:T(8,128)S(1)}, u32[]{:S(2)}, u32[]{:S(2)}) collective-permute-start(f32[4,5,1,8,128]{4,3,1,0,2:T(8,128)S(1)} %bitcast_select_fusion.4), channel_id=1, source_target_pairs={{1,0},{2,1},{3,2},{4,3},{5,4},{6,5},{7,6},{8,7},{9,8},{10,9},{11,1... | collective-permute-start | bytes 245768 | tf_op jit(solution)/shard_map/ppermute | solution.py:25
  131.3 0.2 copy.422
  131.6 0.2 copy.424
  132.1 1.0 collective-permute-done.7
  133.6 0.2 copy.426
  134.0 0.2 copy.428
  134.9 0.2 copy.430
  135.3 0.2 copy.432
  136.3 0.2 copy.434
  136.6 0.2 copy.436
  137.2 0.7 copy-done.8
  137.9 0.7 copy-done.10
  138.6 0.3 fusion.63
  138.8 110.6 %all-reduce.33 = f32[4,512]{1,0:T(4,128)S(1)} all-reduce(f32[4,512]{1,0:T(4,128)S(1)} %fusion.63), channel_id=2, replica_groups=mesh['inst'=8,'space'=64] {'space'}, use_global_device_ids=true, to_apply=%region_58.59.clone | all-reduce | flops 2048 | bytes 16384
  249.5 0.7 constant_dynamic-slice_fusion
  (220 shorter events, 13.4 us)
Async XLA Ops:
  0.6 8.8 %copy-start.3 = (f32[4,5,1,8,128]{4,3,2,1,0:T(8,128)S(1)}, f32[4,5,1,8,128]{4,3,2,1,0:T(8,128)}, u32[]{:S(2)}) copy-start(f32[4,5,1,8,128]{4,3,2,1,0:T(8,128)} %param.11) | copy-start | bytes 245764
  0.6 51.8 %collective-permute-start = (f32[4,5,1,8,128]{4,3,2,1,0:T(8,128)}, f32[4,5,1,8,128]{4,3,2,1,0:T(8,128)S(1)}, u32[]{:S(2)}, u32[]{:S(2)}) collective-permute-start(f32[4,5,1,8,128]{4,3,2,1,0:T(8,128)} %param.11), channel_id=1, source_target_pairs={{0,1},{1,2},{2,3},{3,4},{4,5},{5,6},{6,7},{7,8},{8,9},{9,10},{10,1... | collective-permute-start | bytes 245768 | tf_op jit(solution)/shard_map/ppermute | solution.py:22
  2.7 49.7 %collective-permute-start.1 = (f32[4,5,1,8,128]{4,3,2,1,0:T(8,128)}, f32[4,5,1,8,128]{4,3,2,1,0:T(8,128)S(1)}, u32[]{:S(2)}, u32[]{:S(2)}) collective-permute-start(f32[4,5,1,8,128]{4,3,2,1,0:T(8,128)} %param.11), channel_id=1, source_target_pairs={{1,0},{2,1},{3,2},{4,3},{5,4},{6,5},{7,6},{8,7},{9,8},{10,9},{11,1... | collective-permute-start | bytes 245768 | tf_op jit(solution)/shard_map/ppermute | solution.py:25
  46.5 0.7 copy-start.9
  50.4 0.9 copy-start.1
  50.4 1.0 copy-start.5
  51.4 0.9 copy-start
  52.4 0.9 copy-start.4
  53.3 0.9 copy-start.6
  54.2 0.9 copy-start.2
  59.4 8.7 %collective-permute-start.2 = (f32[4,5,1,8,128]{4,3,1,0,2:T(8,128)S(1)}, f32[4,5,1,8,128]{4,3,1,0,2:T(8,128)S(1)}, u32[]{:S(2)}, u32[]{:S(2)}) collective-permute-start(f32[4,5,1,8,128]{4,3,1,0,2:T(8,128)S(1)} %bitcast_select_fusion.12), channel_id=1, source_target_pairs={{0,1},{1,2},{2,3},{3,4},{4,5},{5,6},{6,7},{7,8},{8,9},{9,10},{10,1... | collective-permute-start | bytes 245768 | tf_op jit(solution)/shard_map/ppermute | solution.py:22
  61.3 7.8 %collective-permute-start.3 = (f32[4,5,1,8,128]{4,3,1,0,2:T(8,128)S(1)}, f32[4,5,1,8,128]{4,3,1,0,2:T(8,128)S(1)}, u32[]{:S(2)}, u32[]{:S(2)}) collective-permute-start(f32[4,5,1,8,128]{4,3,1,0,2:T(8,128)S(1)} %bitcast_select_fusion.12), channel_id=1, source_target_pairs={{1,0},{2,1},{3,2},{4,3},{5,4},{6,5},{7,6},{8,7},{9,8},{10,9},{11,1... | collective-permute-start | bytes 245768 | tf_op jit(solution)/shard_map/ppermute | solution.py:25
  73.4 45.6 %collective-permute-start.4 = (f32[4,5,1,8,128]{4,3,1,0,2:T(8,128)S(1)}, f32[4,5,1,8,128]{4,3,1,0,2:T(8,128)S(1)}, u32[]{:S(2)}, u32[]{:S(2)}) collective-permute-start(f32[4,5,1,8,128]{4,3,1,0,2:T(8,128)S(1)} %fusion.73), channel_id=1, source_target_pairs={{0,1},{1,2},{2,3},{3,4},{4,5},{5,6},{6,7},{7,8},{8,9},{9,10},{10,1... | collective-permute-start | bytes 245768 | tf_op jit(solution)/shard_map/ppermute | solution.py:22
  75.3 43.7 %collective-permute-start.5 = (f32[4,5,1,8,128]{4,3,1,0,2:T(8,128)S(1)}, f32[4,5,1,8,128]{4,3,1,0,2:T(8,128)S(1)}, u32[]{:S(2)}, u32[]{:S(2)}) collective-permute-start(f32[4,5,1,8,128]{4,3,1,0,2:T(8,128)S(1)} %fusion.73), channel_id=1, source_target_pairs={{1,0},{2,1},{3,2},{4,3},{5,4},{6,5},{7,6},{8,7},{9,8},{10,9},{11,1... | collective-permute-start | bytes 245768 | tf_op jit(solution)/shard_map/ppermute | solution.py:25
  123.4 8.7 %collective-permute-start.6 = (f32[4,5,1,8,128]{4,3,1,0,2:T(8,128)S(1)}, f32[4,5,1,8,128]{4,3,1,0,2:T(8,128)S(1)}, u32[]{:S(2)}, u32[]{:S(2)}) collective-permute-start(f32[4,5,1,8,128]{4,3,1,0,2:T(8,128)S(1)} %bitcast_select_fusion.4), channel_id=1, source_target_pairs={{0,1},{1,2},{2,3},{3,4},{4,5},{5,6},{6,7},{7,8},{8,9},{9,10},{10,1... | collective-permute-start | bytes 245768 | tf_op jit(solution)/shard_map/ppermute | solution.py:22
  125.3 7.8 %collective-permute-start.7 = (f32[4,5,1,8,128]{4,3,1,0,2:T(8,128)S(1)}, f32[4,5,1,8,128]{4,3,1,0,2:T(8,128)S(1)}, u32[]{:S(2)}, u32[]{:S(2)}) collective-permute-start(f32[4,5,1,8,128]{4,3,1,0,2:T(8,128)S(1)} %bitcast_select_fusion.4), channel_id=1, source_target_pairs={{1,0},{2,1},{3,2},{4,3},{5,4},{6,5},{7,6},{8,7},{9,8},{10,9},{11,1... | collective-permute-start | bytes 245768 | tf_op jit(solution)/shard_map/ppermute | solution.py:25
  137.2 0.7 copy-start.8
  137.9 112.3 %copy-start.7 = (f32[4,5,1,8,128]{4,3,1,0,2:T(8,128)}, f32[4,5,1,8,128]{4,3,1,0,2:T(8,128)S(1)}, u32[]{:S(2)}) copy-start(f32[4,5,1,8,128]{4,3,1,0,2:T(8,128)S(1)} %fusion.65) | copy-start | bytes 245764
  137.9 0.7 copy-start.10
where the time goes:
time: 251 us; the launch traced here: 250 us
  blocking collectives  182 us (73%)
  starting transfers between devices  30.9 us (12%)
  local copies, waits for them, and re-layouts  24.2 us (10%)
  other arithmetic  5.55 us (2%)
  matrix products  2.61 us (1%)
    unnamed x1, blocking collectives  111 us
    all_gather x2, blocking collectives, on_device(): lax.all_gather(adjoint, 'inst', axis=0, tiled=True)  71.8 us
    ppermute x4, starting transfers between devices, with_halo(): lax.ppermute(lax.slice_in_dim(block, 0, width, axis=dim), axis, backward)  23.1 us
    unnamed x24, local copies, waits for them, and re-layouts  8.25 us
    ppermute x4, starting transfers between devices, with_halo(): lax.ppermute(lax.slice_in_dim(block, block.shape[dim] - width, None, axis...  7.81 us
    slice x33, local copies, waits for them, and re-layouts, coupling(): plus_chord = jnp.roll(values_in, -1, axis=4)  5.23 us
  transfers between devices with their start and end apart: 8, of which 2 were waited for; matrix products, arithmetic and copies ran while one was open for 4% of the time, Pallas kernels for 0%

commit v1 on v0

v1 whole, which is shorter than its diff:
```python
import functools
import math

import jax
import jax.numpy as jnp
from jax import lax
from jax.experimental import pallas as pl
from jax.experimental.pallas import tpu as pltpu
from jax.sharding import PartitionSpec as P

NCOL = 4
PSTEPS = 2
SEC_DEV = 8
GAIN = 0.25
K = 5
MESH = pl.DeviceIdType.MESH


def spectral_row(count):
    row = [0.0]
    for gap in range(1, count):
        sign = 1.0 if gap % 2 == 0 else -1.0
        row.append(GAIN * 0.5 * sign / math.tan(math.pi * gap / count))
    return row


def ring_order(count):
    half = count // 2
    order = [half]
    for step in range(1, half + 1):
        for offset in (half - step, half + step):
            if 0 <= offset < count:
                order.append(offset)
    return order


def kernel(
    sizes,
    a_hbm, g_hbm, d_hbm, p_hbm, js_hbm, jn_hbm, jc_hbm, col_hbm, wall_hbm, own_hbm,
    adj_hbm, sens_ref,
    a_ref, a1_ref, g_ref, col_ref, wall_ref, own_ref, raw,
    dm, pm, jsm, jnm, jcm, ps, pn, pc,
    rs, b_ref, u_ref, h_ref, spec_rx, halo_rx, dest_hot, sec_tx, sec_rx,
    in_sem, spec_tx_sem, spec_rx_sem, halo_tx_sem, halo_rx_sem, sec_sem, out_sem,
):
    members, n_inst, n_space, quads = sizes
    row = spectral_row(members * n_inst)
    inst = lax.axis_index("inst")
    space = lax.axis_index("space")

    spec_peers = [(lax.rem(inst + d, n_inst), space) for d in range(1, n_inst)]
    halo_peers = [(inst, lax.rem(space + 1, n_space)), (inst, lax.rem(space + n_space - 1, n_space))]
    rings = n_space // quads
    zed, quad = space // quads, lax.rem(space, quads)
    sec_peers = []
    for dz in ring_order(rings):
        for dq in range(quads):
            if dz or dq:
                sec_peers.append((inst, lax.rem(zed + dz, rings) * quads + lax.rem(quad + dq, quads)))

    barrier = pltpu.get_barrier_semaphore()
    for peer in spec_peers + sec_peers:
        pl.semaphore_signal(barrier, inc=1, device_id=peer, device_id_type=MESH)
    loads = [
        pltpu.make_async_copy(src, dst, in_sem.at[n])
        for n, (src, dst) in enumerate(
            [
                (a_hbm, a_ref), (g_hbm, g_ref), (col_hbm, col_ref), (wall_hbm, wall_ref), (own_hbm, own_ref),
                (p_hbm, raw.at[0]), (jn_hbm, raw.at[1]), (jc_hbm, raw.at[2]), (js_hbm, raw.at[3]), (d_hbm, raw.at[4]),
            ]
        )
    ]
    for load in loads:
        load.start()
    loads[0].wait()
    pl.semaphore_wait(barrier, len(spec_peers) + len(sec_peers))

    def send_state(step, source):
        spec = []
        for e, peer in enumerate(spec_peers):
            copy = pltpu.make_async_remote_copy(
                src_ref=source, dst_ref=spec_rx.at[step, e], send_sem=spec_tx_sem.at[step, e],
                recv_sem=spec_rx_sem.at[step, e], device_id=peer, device_id_type=MESH,
            )
            copy.start()
            spec.append(copy)
        return spec

    def send_halo(slot, source):
        halo = []
        for side, peer in enumerate(halo_peers):
            copy = pltpu.make_async_remote_copy(
                src_ref=source, dst_ref=halo_rx.at[slot, side], send_sem=halo_tx_sem.at[slot, side],
                recv_sem=halo_rx_sem.at[slot, side], device_id=peer, device_id_type=MESH,
            )
            copy.start()
            halo.append(copy)
        return halo

    def block(ref, m, k, l):
        at = (m * K * K + k * K + l) * 8
        if not isinstance(at, int):
            at = pl.multiple_of(at, 8)
        return ref[pl.ds(at, 8), :]

    lane_row = lax.broadcasted_iota(jnp.int32, (8, 128), 0)

    def normal_diff(v):
        minus = jnp.where(lane_row > 0, pltpu.roll(v, 1, 0), 0.0)
        plus = jnp.where(lane_row < 7, pltpu.roll(v, 7, 0), 0.0)
        return minus - plus

    def chord_diff(v):
        return pltpu.roll(v, 1, 1) - pltpu.roll(v, 127, 1)

    def span_diff(slot, m, l):
        minus = jnp.where(space > 0, halo_rx[slot, 0, m, l], 0.0)
        plus = jnp.where(space < n_space - 1, halo_rx[slot, 1, m, l], 0.0)
        return minus - plus

    state = a_ref
    halo_a = send_halo(0, state)
    spec = send_state(0, state)

    for load in loads[1:]:
        load.wait()
    rows = members * K * K * 8
    part = 160
    for n, wide in enumerate((pm, jnm, jcm, jsm, dm)):
        @pl.loop(0, rows // part)
        def _(i, n=n, wide=wide):
            at = pl.multiple_of(i * part, part)
            wide[pl.ds(at, part), :] = raw[n, pl.ds(at, part), :].astype(jnp.float32)

    @pl.loop(0, members)
    def _(m):
        for jac, product in ((jnm, pn), (jcm, pc), (jsm, ps)):
            right = [[0.5 * block(jac, m, j, l) for l in range(K)] for j in range(K)]
            for k in range(K):
                left = [block(pm, m, k, j) for j in range(K)]
                for l in range(K):
                    total = left[0] * right[0][l]
                    for j in range(1, K):
                        total = total + left[j] * right[j][l]
                    at = pl.multiple_of((m * K * K + k * K + l) * 8, 8)
                    product[pl.ds(at, 8), :] = total

    owner = own_ref[...]
    dest_hot[...] = jnp.where(
        lax.broadcasted_iota(jnp.int32, (n_space, 128), 0) == jnp.broadcast_to(owner // SEC_DEV, (n_space, 128)), 1.0, 0.0
    ).astype(jnp.bfloat16)
    sec_tx[...] = jnp.zeros_like(sec_tx)
    colour = col_ref[...]

    for step in range(PSTEPS):
        @pl.loop(0, members)
        def _(m, state=state):
            v = [state[m, l] for l in range(K)]
            dn = [normal_diff(v[l]) for l in range(K)]
            dc = [chord_diff(v[l]) for l in range(K)]
            for k in range(K):
                local = block(dm, m, k, 0) * v[0]
                cross = block(jnm, m, k, 0) * dn[0] + block(jcm, m, k, 0) * dc[0]
                for l in range(1, K):
                    local = local + block(dm, m, k, l) * v[l]
                    cross = cross + (block(jnm, m, k, l) * dn[l] + block(jcm, m, k, l) * dc[l])
                rs[m, k] = g_ref[m, k] - (local + 0.5 * cross)

        def add_block(d, source):
            for k in range(K):
                v = [source[j, k] for j in range(members)]
                for m in range(members):
                    total = rs[m, k]
                    for j in range(members):
                        weight = row[(members * d + j - m) % len(row)]
                        if weight:
                            total = total - weight * v[j]
                    rs[m, k] = total

        add_block(0, state)
        for copy in halo_a:
            copy.wait_recv()

        @pl.loop(0, members)
        def _(m, step=step):
            ds = [span_diff(2 * step, m, l) for l in range(K)]
            for k in range(K):
                cross = block(jsm, m, k, 0) * ds[0]
                for l in range(1, K):
                    cross = cross + block(jsm, m, k, l) * ds[l]
                rs[m, k] = rs[m, k] - 0.5 * cross

        for e, copy in enumerate(spec):
            copy.wait_recv()
            add_block(n_inst - 1 - e, spec_rx.at[step, e])

        for m in range(members):
            r = [rs[m, l] for l in range(K)]
            for k in range(K):
                total = block(pm, m, k, 0) * r[0]
                for l in range(1, K):
                    total = total + block(pm, m, k, l) * r[l]
                b_ref[m, k] = total
                u_ref[m, k] = jnp.where(colour == 0, total, 0.0)

        def cross_terms(m, source):
            v = [source[m, l] for l in range(K)]
            dn = [normal_diff(v[l]) for l in range(K)]
            dc = [chord_diff(v[l]) for l in range(K)]
            out = []
            for k in range(K):
                total = block(pn, m, k, 0) * dn[0] + block(pc, m, k, 0) * dc[0]
                for l in range(1, K):
                    total = total + (block(pn, m, k, l) * dn[l] + block(pc, m, k, l) * dc[l])
                out.append(total)
            return v, out

        @pl.loop(1, NCOL)
        def _(value):
            mine = colour == value
            for m in range(members):
                v, cross = cross_terms(m, u_ref)
                for k in range(K):
                    u_ref[m, k] = jnp.where(mine, b_ref[m, k] - cross[k], v[k])

        halo_u = send_halo(2 * step + 1, u_ref)
        for m in range(members):
            _, cross = cross_terms(m, u_ref)
            for k in range(K):
                rs[m, k] = cross[k]
        for copy in halo_u:
            copy.wait_recv()
        for m in range(members):
            ds = [span_diff(2 * step + 1, m, l) for l in range(K)]
            for k in range(K):
                total = b_ref[m, k]
                for l in range(K):
                    total = total - block(ps, m, k, l) * ds[l]
                b_ref[m, k] = total
                h_ref[m, k] = jnp.where(colour == NCOL - 1, total - rs[m, k], u_ref[m, k])

        @pl.loop(1, NCOL)
        def _(back):
            mine = colour == NCOL - 1 - back
            for m in range(members):
                v, cross = cross_terms(m, h_ref)
                for k in range(K):
                    h_ref[m, k] = jnp.where(mine, b_ref[m, k] - cross[k], v[k])

        sent = spec + halo_a + halo_u
        if step < PSTEPS - 1:
            for m in range(members):
                for k in range(K):
                    a1_ref[m, k] = state[m, k] + h_ref[m, k]
            halo_a = send_halo(2 * step + 2, a1_ref)
            spec = send_state(step + 1, a1_ref)
            state = a1_ref
        else:
            for m in range(members):
                for k in range(K):
                    h_ref[m, k] = state[m, k] + h_ref[m, k]
        for copy in sent:
            copy.wait_send()

    sub = lax.broadcasted_iota(jnp.int32, (SEC_DEV, 128), 0)
    inner = jnp.broadcast_to(lax.rem(owner, SEC_DEV), (SEC_DEV, 128))
    shares = []
    for m in range(members):
        wall = wall_ref[m, 0] * h_ref[m, 0][0:1, :]
        for k in range(1, K):
            wall = wall + wall_ref[m, k] * h_ref[m, k][0:1, :]
        shares.append(jnp.where(sub == inner, jnp.broadcast_to(wall, (SEC_DEV, 128)), 0.0))
    share = jnp.concatenate(shares, axis=0)
    high = share.astype(jnp.bfloat16)
    rest = share - high.astype(jnp.float32)
    middle = rest.astype(jnp.bfloat16)
    low = (rest - middle.astype(jnp.float32)).astype(jnp.bfloat16)
    hot = dest_hot[...]
    sums = lax.dot_general(
        jnp.concatenate([hot, hot, hot], axis=1),
        jnp.concatenate([high, middle, low], axis=1),
        (((1,), (1,)), ((), ())),
        preferred_element_type=jnp.float32,
    )
    width = members * SEC_DEV
    for n in range(n_space):
        sec_tx[n, :, 0:width] = sums[n : n + 1, :]
    for e, peer in enumerate(sec_peers):
        pltpu.make_async_remote_copy(
            src_ref=sec_tx.at[peer[1]], dst_ref=sec_rx.at[e], send_sem=sec_sem.at[0],
            recv_sem=sec_sem.at[1], device_id=peer, device_id_type=MESH,
        ).start()
    write = pltpu.make_async_copy(h_ref, adj_hbm, out_sem)
    write.start()
    every = pltpu.make_async_remote_copy(
        src_ref=sec_tx.at[pl.ds(0, len(sec_peers))], dst_ref=sec_rx, send_sem=sec_sem.at[0],
        recv_sem=sec_sem.at[1], device_id=sec_peers[0], device_id_type=MESH,
    )
    own_share = sec_tx[space]
    every.wait_recv()
    parts = [own_share] + [sec_rx[e] for e in range(len(sec_peers))]
    while len(parts) > 1:
        parts = [parts[n] + parts[n + 1] if n + 1 < len(parts) else parts[n] for n in range(0, len(parts), 2)]
    for m in range(members):
        at = (128 - m * SEC_DEV) % 128
        line = pltpu.roll(parts[0], at, 1) if at else parts[0]
        sens_ref[m : m + 1, :] = line[:, 0:SEC_DEV]
    every.wait_send()
    write.wait()


def on_device(sizes, a, g, d, p, js, jn, jc, colour, wall, owner):
    members, n_inst, n_space, quads = sizes
    field = (members, K, 8, 128)
    flat = (members * K * K * 8, 128)
    vmem, f32 = pltpu.VMEM, jnp.float32
    n_spec, n_sec = n_inst - 1, n_space - 1
    any_spec = pl.BlockSpec(memory_space=pl.ANY)
    adj, sens = pl.pallas_call(
        functools.partial(kernel, sizes),
        out_shape=(jax.ShapeDtypeStruct(field, f32), jax.ShapeDtypeStruct((members, SEC_DEV), f32)),
        in_specs=[any_spec] * 10,
        out_specs=(any_spec, pl.BlockSpec(memory_space=pltpu.VMEM)),
        scratch_shapes=[
            vmem(field, f32), vmem(field, f32), vmem(field, f32),
            vmem((8, 128), jnp.int32), vmem((members, K, 1, 128), f32), vmem((1, 128), jnp.int32),
            vmem((5,) + flat, jnp.bfloat16),
            *[vmem(flat, f32) for _ in range(8)],
            *[vmem(field, f32) for _ in range(4)],
            vmem((PSTEPS, n_spec) + field, f32),
            vmem((2 * PSTEPS, 2) + field, f32),
            vmem((n_space, 128), jnp.bfloat16),
            vmem((n_space, 1, 128), f32),
            vmem((n_sec, 1, 128), f32),
            pltpu.SemaphoreType.DMA((10,)),
            pltpu.SemaphoreType.DMA((PSTEPS, n_spec)),
            pltpu.SemaphoreType.DMA((PSTEPS, n_spec)),
            pltpu.SemaphoreType.DMA((2 * PSTEPS, 2)),
            pltpu.SemaphoreType.DMA((2 * PSTEPS, 2)),
            pltpu.SemaphoreType.DMA((2,)),
            pltpu.SemaphoreType.DMA,
        ],
        compiler_params=pltpu.CompilerParams(
            collective_id=0, has_side_effects=True, vmem_limit_bytes=40 * 1024 * 1024
        ),
        name="adjoint",
    )(
        a.reshape(field), g.reshape(field), *[x.reshape(flat) for x in (d, p, js, jn, jc)],
        colour.reshape(8, 128), wall, owner,
    )
    return adj.reshape(a.shape), sens


def solution(mesh):
    n_inst, n_space = mesh.shape["inst"], mesh.shape["space"]
    sizes = (32 // n_inst, n_inst, n_space, 4)
    return jax.shard_map(
        functools.partial(on_device, sizes),
        mesh=mesh,
        in_specs=(
            P("inst", None, "space", None, None),
            P("inst", None, "space", None, None),
            P("inst", None, None, "space", None, None),
            P("inst", None, None, "space", None, None),
            P("inst", None, None, "space", None, None),
            P("inst", None, None, "space", None, None),
            P("inst", None, None, "space", None, None),
            P("space", None, None),
            P("inst", None, "space", None),
            P("space", None),
        ),
        out_specs=(P("inst", None, "space", None, None), P("inst", "space")),
        check_vma=False,
    )
```

time: 251 us -> 65.5 us (0.26)
  the two profiles are of different devices: /device:TPU:256 before, /device:TPU:1 now
where the time goes in v1:
time: 65.5 us; the launch traced here: 65.1 us
  Pallas kernels  56.2 us (86%)
  local copies, waits for them, and re-layouts  8.32 us (13%)
  between operations  0.67 us (1%)
    pallas_call x1, Pallas kernels, on_device(): pl.pallas_call(functools.partial(kernel, sizes), out_shape=(jax.ShapeDtyp...  56.2 us
    unnamed x22, local copies, waits for them, and re-layouts  8.32 us

profile of v1, /device:TPU:1, one launch (start us, length us, event | category | flops | bytes accessed | tf_op | source)
XLA Modules:
  0.0 65.1 jit_solution(12588918979815385919)
XLA Ops:
  0.6 0.0 copy-start.7
  0.6 0.0 copy-start.8
  0.7 0.0 copy-start.9
  0.7 0.7 %copy-done.7 = f32[4,5,1,128]{3,2,1,0:T(1,128)S(1)} copy-done((f32[4,5,1,128]{3,2,1,0:T(1,128)S(1)}, f32[4,5,1,128]{3,2,1,0:T(1,128)}, u32[]{:S(2)}) %copy-start.7) | copy-done | bytes 10264
  1.3 0.0 copy-done.8
  1.3 0.0 copy-done.9
  1.3 0.0 copy-start
  1.3 0.9 %copy-done = bf16[4,5,5,1,8,128]{5,4,3,2,1,0:T(8,128)(2,1)S(1)} copy-done((bf16[4,5,5,1,8,128]{5,4,3,2,1,0:T(8,128)(2,1)S(1)}, bf16[4,5,5,1,8,128]{5,4,3,2,1,0:T(8,128)(2,1)}, u32[]{:S(2)}) %copy-start) | copy-done | bytes 204824
  2.3 0.0 copy-start.1
  2.3 0.9 %copy-done.1 = bf16[4,5,5,1,8,128]{5,4,3,2,1,0:T(8,128)(2,1)S(1)} copy-done((bf16[4,5,5,1,8,128]{5,4,3,2,1,0:T(8,128)(2,1)S(1)}, bf16[4,5,5,1,8,128]{5,4,3,2,1,0:T(8,128)(2,1)}, u32[]{:S(2)}) %copy-start.1) | copy-done | bytes 204824
  3.2 0.0 copy-start.2
  3.2 0.9 %copy-done.2 = bf16[4,5,5,1,8,128]{5,4,3,2,1,0:T(8,128)(2,1)S(1)} copy-done((bf16[4,5,5,1,8,128]{5,4,3,2,1,0:T(8,128)(2,1)S(1)}, bf16[4,5,5,1,8,128]{5,4,3,2,1,0:T(8,128)(2,1)}, u32[]{:S(2)}) %copy-start.2) | copy-done | bytes 204824
  4.1 0.0 copy-start.3
  4.1 0.9 %copy-done.3 = bf16[4,5,5,1,8,128]{5,4,3,2,1,0:T(8,128)(2,1)S(1)} copy-done((bf16[4,5,5,1,8,128]{5,4,3,2,1,0:T(8,128)(2,1)S(1)}, bf16[4,5,5,1,8,128]{5,4,3,2,1,0:T(8,128)(2,1)}, u32[]{:S(2)}) %copy-start.3) | copy-done | bytes 204824
  5.1 0.0 copy-start.4
  5.1 0.9 %copy-done.4 = bf16[4,5,5,1,8,128]{5,4,3,2,1,0:T(8,128)(2,1)S(1)} copy-done((bf16[4,5,5,1,8,128]{5,4,3,2,1,0:T(8,128)(2,1)S(1)}, bf16[4,5,5,1,8,128]{5,4,3,2,1,0:T(8,128)(2,1)}, u32[]{:S(2)}) %copy-start.4) | copy-done | bytes 204824
  6.0 0.0 copy-start.5
  6.0 0.9 %copy-done.5 = f32[4,5,1,8,128]{4,3,2,1,0:T(8,128)S(1)} copy-done((f32[4,5,1,8,128]{4,3,2,1,0:T(8,128)S(1)}, f32[4,5,1,8,128]{4,3,2,1,0:T(8,128)}, u32[]{:S(2)}) %copy-start.5) | copy-done | bytes 81944
  6.9 0.0 copy-start.6
  6.9 0.9 %copy-done.6 = f32[4,5,1,8,128]{4,3,2,1,0:T(8,128)S(1)} copy-done((f32[4,5,1,8,128]{4,3,2,1,0:T(8,128)S(1)}, f32[4,5,1,8,128]{4,3,2,1,0:T(8,128)}, u32[]{:S(2)}) %copy-start.6) | copy-done | bytes 81944
  7.8 56.2 %adjoint.1 = (f32[4,5,8,128]{3,2,1,0:T(8,128)S(1)}, f32[4,8]{1,0:T(4,128)S(1)}) custom-call(f32[4,5,8,128]{3,2,1,0:T(8,128)S(1)} %bitcast.16, f32[4,5,8,128]{3,2,1,0:T(8,128)S(1)} %bitcast.17, bf16[800,128]{1,0:T(8,128)(2,1)S(1)} %bitcast.11, bf16[800,128]{1,0:T(8,128)(2,1)S(1)} %bitcast.12, bf16[800,128]{1,0:T(8,128)(2,1)S(1)} %bitcast.13, ...), custom_call_target="tpu_custom_call" | custom-call | tf_op jit(solution)/shard_map/adjoint/pallas_call | solution.py:319
  63.9 0.6 copy.15
  64.6 0.6 copy.16
Async XLA Ops:
  0.6 0.7 %copy-start.7 = (f32[4,5,1,128]{3,2,1,0:T(1,128)S(1)}, f32[4,5,1,128]{3,2,1,0:T(1,128)}, u32[]{:S(2)}) copy-start(f32[4,5,1,128]{3,2,1,0:T(1,128)} %wall_hbm.1) | copy-start | bytes 30724
  0.6 0.7 %copy-start.8 = (s32[1,8,128]{2,1,0:T(8,128)S(1)}, s32[1,8,128]{2,1,0:T(8,128)}, u32[]{:S(2)}) copy-start(s32[1,8,128]{2,1,0:T(8,128)} %param.17) | copy-start | bytes 12292
  0.7 0.7 %copy-start.9 = (s32[1,128]{1,0:T(1,128)S(1)}, s32[1,128]{1,0:T(1,128)}, u32[]{:S(2)}) copy-start(s32[1,128]{1,0:T(1,128)} %own_hbm.1) | copy-start | bytes 1540
  1.3 0.9 %copy-start = (bf16[4,5,5,1,8,128]{5,4,3,2,1,0:T(8,128)(2,1)S(1)}, bf16[4,5,5,1,8,128]{5,4,3,2,1,0:T(8,128)(2,1)}, u32[]{:S(2)}) copy-start(bf16[4,5,5,1,8,128]{5,4,3,2,1,0:T(8,128)(2,1)} %param.12) | copy-start | bytes 614404
  2.3 0.9 %copy-start.1 = (bf16[4,5,5,1,8,128]{5,4,3,2,1,0:T(8,128)(2,1)S(1)}, bf16[4,5,5,1,8,128]{5,4,3,2,1,0:T(8,128)(2,1)}, u32[]{:S(2)}) copy-start(bf16[4,5,5,1,8,128]{5,4,3,2,1,0:T(8,128)(2,1)} %param.13) | copy-start | bytes 614404
  3.2 0.9 %copy-start.2 = (bf16[4,5,5,1,8,128]{5,4,3,2,1,0:T(8,128)(2,1)S(1)}, bf16[4,5,5,1,8,128]{5,4,3,2,1,0:T(8,128)(2,1)}, u32[]{:S(2)}) copy-start(bf16[4,5,5,1,8,128]{5,4,3,2,1,0:T(8,128)(2,1)} %param.14) | copy-start | bytes 614404
  4.1 0.9 %copy-start.3 = (bf16[4,5,5,1,8,128]{5,4,3,2,1,0:T(8,128)(2,1)S(1)}, bf16[4,5,5,1,8,128]{5,4,3,2,1,0:T(8,128)(2,1)}, u32[]{:S(2)}) copy-start(bf16[4,5,5,1,8,128]{5,4,3,2,1,0:T(8,128)(2,1)} %param.15) | copy-start | bytes 614404
  5.1 0.9 %copy-start.4 = (bf16[4,5,5,1,8,128]{5,4,3,2,1,0:T(8,128)(2,1)S(1)}, bf16[4,5,5,1,8,128]{5,4,3,2,1,0:T(8,128)(2,1)}, u32[]{:S(2)}) copy-start(bf16[4,5,5,1,8,128]{5,4,3,2,1,0:T(8,128)(2,1)} %param.16) | copy-start | bytes 614404
  6.0 0.9 %copy-start.5 = (f32[4,5,1,8,128]{4,3,2,1,0:T(8,128)S(1)}, f32[4,5,1,8,128]{4,3,2,1,0:T(8,128)}, u32[]{:S(2)}) copy-start(f32[4,5,1,8,128]{4,3,2,1,0:T(8,128)} %param.10) | copy-start | bytes 245764
  6.9 0.9 %copy-start.6 = (f32[4,5,1,8,128]{4,3,2,1,0:T(8,128)S(1)}, f32[4,5,1,8,128]{4,3,2,1,0:T(8,128)}, u32[]{:S(2)}) copy-start(f32[4,5,1,8,128]{4,3,2,1,0:T(8,128)} %param.11) | copy-start | bytes 245764

commit v2 on v1

--- a/solution.py
+++ b/solution.py
@@ -13,6 +13,7 @@
 SEC_DEV = 8
 GAIN = 0.25
 K = 5
+GATHER, SCATTER = (0, 1), (2, 3, 4)
 MESH = pl.DeviceIdType.MESH
 
 
@@ -37,18 +38,21 @@
 def kernel(
     sizes,
     a_hbm, g_hbm, d_hbm, p_hbm, js_hbm, jn_hbm, jc_hbm, col_hbm, wall_hbm, own_hbm,
-    adj_hbm, sens_ref,
+    adj_ref, sens_ref,
     a_ref, a1_ref, g_ref, col_ref, wall_ref, own_ref, raw,
     dm, pm, jsm, jnm, jcm, ps, pn, pc,
-    rs, b_ref, u_ref, h_ref, spec_rx, halo_rx, dest_hot, sec_tx, sec_rx,
-    in_sem, spec_tx_sem, spec_rx_sem, halo_tx_sem, halo_rx_sem, sec_sem, out_sem,
+    rs, b_ref, u_ref, h_ref, ya_rx, xa_tx, xa_rx, xb_rx, yb_tx, yb_rx, halo_rx, dest_hot, sec_tx, sec_rx,
+    in_sem, ya_sem, xa_sem, xb_sem, yb_sem, halo_tx_sem, halo_rx_sem, sec_sem, known_sem,
 ):
     members, n_inst, n_space, quads = sizes
     row = spectral_row(members * n_inst)
     inst = lax.axis_index("inst")
     space = lax.axis_index("space")
 
-    spec_peers = [(lax.rem(inst + d, n_inst), space) for d in range(1, n_inst)]
+    side = n_inst // 2
+    high, why = inst // side, lax.rem(inst, side)
+    y_peers = [(high * side + lax.rem(why + d, side), space) for d in range(1, side)]
+    x_peer = (lax.rem(inst + side, n_inst), space)
     halo_peers = [(inst, lax.rem(space + 1, n_space)), (inst, lax.rem(space + n_space - 1, n_space))]
     rings = n_space // quads
     zed, quad = space // quads, lax.rem(space, quads)
@@ -59,7 +63,8 @@
                 sec_peers.append((inst, lax.rem(zed + dz, rings) * quads + lax.rem(quad + dq, quads)))
 
     barrier = pltpu.get_barrier_semaphore()
-    for peer in spec_peers + sec_peers:
+    near = y_peers + [x_peer] + halo_peers
+    for peer in near:
         pl.semaphore_signal(barrier, inc=1, device_id=peer, device_id_type=MESH)
     loads = [
         pltpu.make_async_copy(src, dst, in_sem.at[n])
@@ -72,19 +77,118 @@
     ]
     for load in loads:
         load.start()
-    loads[0].wait()
-    pl.semaphore_wait(barrier, len(spec_peers) + len(sec_peers))
-
-    def send_state(step, source):
-        spec = []
-        for e, peer in enumerate(spec_peers):
-            copy = pltpu.make_async_remote_copy(
-                src_ref=source, dst_ref=spec_rx.at[step, e], send_sem=spec_tx_sem.at[step, e],
-                recv_sem=spec_rx_sem.at[step, e], device_id=peer, device_id_type=MESH,
+    for load in loads:
+        load.wait()
+    rows = members * K * K * 8
+    part = 160
+    for n, wide in enumerate((pm, jnm, jcm, jsm, dm)):
+        @pl.loop(0, rows // part)
+        def _(i, n=n, wide=wide):
+            at = pl.multiple_of(i * part, part)
+            wide[pl.ds(at, part), :] = raw[n, pl.ds(at, part), :].astype(jnp.float32)
+
+    pl.semaphore_wait(barrier, len(near))
+
+    def remote(source, target, sems, index, peer):
+        copy = pltpu.make_async_remote_copy(
+            src_ref=source, dst_ref=target, send_sem=sems.at[(0,) + index], recv_sem=sems.at[(1,) + index],
+            device_id=peer, device_id_type=MESH,
+        )
+        copy.start()
+        return copy
+
+    def weight(offset, moved):
+        one, two = row[offset % len(row)], row[(offset + len(row) // 2) % len(row)]
+        return jnp.where(moved, jnp.float32(two), jnp.float32(one))
+
+    spread = range(1 - members, members)
+    from_weight, from_pair, to_weight, to_pair = {}, {}, {}, {}
+    for d in range(1, side):
+        for gap in spread:
+            offset = gap - members * d
+            half = len(row) // 2
+            from_weight[d, gap] = weight(offset, why < d)
+            from_pair[d, gap] = weight(offset + half, why < d)
+            to_weight[d, gap] = weight(offset, why >= side - d)
+            to_pair[d, gap] = weight(offset + half, why >= side - d)
+
+    def near_sum(v, m, shift, total=None):
+        for j in range(members):
+            entry = row[(j - m + shift) % len(row)]
+            if entry:
+                total = entry * v[j] if total is None else total + entry * v[j]
+        return total
+
+    def spectral_start(step, source):
+        copies = {}
+        for k in SCATTER:
+            copies["xb", k] = remote(source.at[:, k], xb_rx.at[step, k], xb_sem, (step, k), x_peer)
+        for k in GATHER:
+            for d, peer in enumerate(y_peers):
+                copies["ya", k, d] = remote(source.at[:, k], ya_rx.at[step, d, k], ya_sem, (step, d, k), peer)
+        return copies
+
+    def spectral_own(source):
+        for k in range(K):
+            v = [source[j, k] for j in range(members)]
+            for m in range(members):
+                rs[m, k] = rs[m, k] - near_sum(v, m, 0)
+
+    def spectral_middle(step, source, copies):
+        half = len(row) // 2
+        for k in SCATTER:
+            v = [source[j, k] for j in range(members)]
+            copies["xb", k].wait_recv()
+            w = [xb_rx[step, k, j] for j in range(members)]
+            for d in range(1, side):
+                for m in range(members):
+                    total = to_weight[d, -m] * v[0] + to_pair[d, -m] * w[0]
+                    for j in range(1, members):
+                        total = total + (to_weight[d, j - m] * v[j] + to_pair[d, j - m] * w[j])
+                    yb_tx[step, d - 1, k, m] = total
+                copies["yb", k, d - 1] = remote(
+                    yb_tx.at[step, d - 1, k], yb_rx.at[step, d - 1, k], yb_sem, (step, d - 1, k), y_peers[d - 1]
+                )
+            for m in range(members):
+                rs[m, k] = rs[m, k] - near_sum(w, m, half)
+        for k in GATHER:
+            for d in range(side - 1):
+                copies["ya", k, d].wait_recv()
+            v = [source[j, k] for j in range(members)]
+            others = [[ya_rx[step, d, k, j] for j in range(members)] for d in range(side - 1)]
+            for m in range(members):
+                total = near_sum(v, m, half)
+                for d in range(1, side):
+                    for j in range(members):
+                        total = total + from_pair[d, j - m] * others[d - 1][j]
+                xa_tx[step, k, m] = total
+            copies["xa", k] = remote(xa_tx.at[step, k], xa_rx.at[step, k], xa_sem, (step, k), x_peer)
+            for m in range(members):
+                total = rs[m, k]
+                for d in range(1, side):
+                    for j in range(members):
+                        total = total - from_weight[d, j - m] * others[d - 1][j]
+                rs[m, k] = total
+
+    def spectral_end(step, copies):
+        for k in GATHER:
+            copies["xa", k].wait_recv()
+            for m in range(members):
+                rs[m, k] = rs[m, k] - xa_rx[step, k, m]
+        for k in SCATTER:
+            for d in range(side - 1):
+                copies["yb", k, d].wait_recv()
+            for m in range(members):
+                rs[m, k] = rs[m, k] - (yb_rx[step, 0, k, m] + yb_rx[step, 1, k, m] + yb_rx[step, 2, k, m])
+
+    def tell(turn):
+        for far in (1 << turn, n_space - (1 << turn)):
+            pl.semaphore_signal(
+                known_sem.at[turn], inc=1, device_id=(inst, lax.rem(space + far, n_space)), device_id_type=MESH
             )
-            copy.start()
-            spec.append(copy)
-        return spec
+
+    def learn(turn):
+        pl.semaphore_wait(known_sem.at[turn], 2)
 
     def send_halo(slot, source):
         halo = []
@@ -118,32 +222,24 @@
         plus = jnp.where(space < n_space - 1, halo_rx[slot, 1, m, l], 0.0)
         return minus - plus
 
+    def fold():
+        @pl.loop(0, members)
+        def _(m):
+            for jac, product in ((jnm, pn), (jcm, pc), (jsm, ps)):
+                right = [[0.5 * block(jac, m, j, l) for l in range(K)] for j in range(K)]
+                for k in range(K):
+                    left = [block(pm, m, k, j) for j in range(K)]
+                    for l in range(K):
+                        total = left[0] * right[0][l]
+                        for j in range(1, K):
+                            total = total + left[j] * right[j][l]
+                        at = pl.multiple_of((m * K * K + k * K + l) * 8, 8)
+                        product[pl.ds(at, 8), :] = total
+
     state = a_ref
+    spec = spectral_start(0, state)
     halo_a = send_halo(0, state)
-    spec = send_state(0, state)
-
-    for load in loads[1:]:
-        load.wait()
-    rows = members * K * K * 8
-    part = 160
-    for n, wide in enumerate((pm, jnm, jcm, jsm, dm)):
-        @pl.loop(0, rows // part)
-        def _(i, n=n, wide=wide):
-            at = pl.multiple_of(i * part, part)
-            wide[pl.ds(at, part), :] = raw[n, pl.ds(at, part), :].astype(jnp.float32)
-
-    @pl.loop(0, members)
-    def _(m):
-        for jac, product in ((jnm, pn), (jcm, pc), (jsm, ps)):
-            right = [[0.5 * block(jac, m, j, l) for l in range(K)] for j in range(K)]
-            for k in range(K):
-                left = [block(pm, m, k, j) for j in range(K)]
-                for l in range(K):
-                    total = left[0] * right[0][l]
-                    for j in range(1, K):
-                        total = total + left[j] * right[j][l]
-                    at = pl.multiple_of((m * K * K + k * K + l) * 8, 8)
-                    product[pl.ds(at, 8), :] = total
+    tell(0)
 
     owner = own_ref[...]
     dest_hot[...] = jnp.where(
@@ -166,18 +262,10 @@
                     cross = cross + (block(jnm, m, k, l) * dn[l] + block(jcm, m, k, l) * dc[l])
                 rs[m, k] = g_ref[m, k] - (local + 0.5 * cross)
 
-        def add_block(d, source):
-            for k in range(K):
-                v = [source[j, k] for j in range(members)]
-                for m in range(members):
-                    total = rs[m, k]
-                    for j in range(members):
-                        weight = row[(members * d + j - m) % len(row)]
-                        if weight:
-                            total = total - weight * v[j]
-                    rs[m, k] = total
-
-        add_block(0, state)
+        spectral_own(state)
+        spectral_middle(step, state, spec)
+        if step == 0:
+            fold()
         for copy in halo_a:
             copy.wait_recv()
 
@@ -190,9 +278,9 @@
                     cross = cross + block(jsm, m, k, l) * ds[l]
                 rs[m, k] = rs[m, k] - 0.5 * cross
 
-        for e, copy in enumerate(spec):
-            copy.wait_recv()
-            add_block(n_inst - 1 - e, spec_rx.at[step, e])
+        learn(3 * step)
+        tell(3 * step + 1)
+        spectral_end(step, spec)
 
         for m in range(members):
             r = [rs[m, l] for l in range(K)]
@@ -228,6 +316,9 @@
             _, cross = cross_terms(m, u_ref)
             for k in range(K):
                 rs[m, k] = cross[k]
+        if step == 0:
+            learn(1)
+            tell(2)
         for copy in halo_u:
             copy.wait_recv()
         for m in range(members):
@@ -247,18 +338,20 @@
                 for k in range(K):
                     h_ref[m, k] = jnp.where(mine, b_ref[m, k] - cross[k], v[k])
 
-        sent = spec + halo_a + halo_u
+        sent = list(spec.values()) + halo_a + halo_u
         if step < PSTEPS - 1:
             for m in range(members):
                 for k in range(K):
                     a1_ref[m, k] = state[m, k] + h_ref[m, k]
+            spec = spectral_start(step + 1, a1_ref)
             halo_a = send_halo(2 * step + 2, a1_ref)
-            spec = send_state(step + 1, a1_ref)
             state = a1_ref
+            learn(2)
+            tell(3)
         else:
             for m in range(members):
                 for k in range(K):
-                    h_ref[m, k] = state[m, k] + h_ref[m, k]
+                    adj_ref[m, k] = state[m, k] + h_ref[m, k]
         for copy in sent:
             copy.wait_send()
 
@@ -266,9 +359,9 @@
     inner = jnp.broadcast_to(lax.rem(owner, SEC_DEV), (SEC_DEV, 128))
     shares = []
     for m in range(members):
-        wall = wall_ref[m, 0] * h_ref[m, 0][0:1, :]
+        wall = wall_ref[m, 0] * adj_ref[m, 0][0:1, :]
         for k in range(1, K):
-            wall = wall + wall_ref[m, k] * h_ref[m, k][0:1, :]
+            wall = wall + wall_ref[m, k] * adj_ref[m, k][0:1, :]
         shares.append(jnp.where(sub == inner, jnp.broadcast_to(wall, (SEC_DEV, 128)), 0.0))
     share = jnp.concatenate(shares, axis=0)
     high = share.astype(jnp.bfloat16)
@@ -285,13 +378,12 @@
     width = members * SEC_DEV
     for n in range(n_space):
         sec_tx[n, :, 0:width] = sums[n : n + 1, :]
+    learn(4)
     for e, peer in enumerate(sec_peers):
         pltpu.make_async_remote_copy(
             src_ref=sec_tx.at[peer[1]], dst_ref=sec_rx.at[e], send_sem=sec_sem.at[0],
             recv_sem=sec_sem.at[1], device_id=peer, device_id_type=MESH,
         ).start()
-    write = pltpu.make_async_copy(h_ref, adj_hbm, out_sem)
-    write.start()
     every = pltpu.make_async_remote_copy(
         src_ref=sec_tx.at[pl.ds(0, len(sec_peers))], dst_ref=sec_rx, send_sem=sec_sem.at[0],
         recv_sem=sec_sem.at[1], device_id=sec_peers[0], device_id_type=MESH,
@@ -306,7 +398,6 @@
         line = pltpu.roll(parts[0], at, 1) if at else parts[0]
         sens_ref[m : m + 1, :] = line[:, 0:SEC_DEV]
     every.wait_send()
-    write.wait()
 
 
 def on_device(sizes, a, g, d, p, js, jn, jc, colour, wall, owner):
@@ -314,34 +405,38 @@
     field = (members, K, 8, 128)
     flat = (members * K * K * 8, 128)
     vmem, f32 = pltpu.VMEM, jnp.float32
-    n_spec, n_sec = n_inst - 1, n_space - 1
-    any_spec = pl.BlockSpec(memory_space=pl.ANY)
+    lump, side, n_sec = (members, 8, 128), n_inst // 2, n_space - 1
+    hbm_spec = pl.BlockSpec(memory_space=pltpu.HBM)
     adj, sens = pl.pallas_call(
         functools.partial(kernel, sizes),
-        out_shape=(jax.ShapeDtypeStruct(field, f32), jax.ShapeDtypeStruct((members, SEC_DEV), f32)),
-        in_specs=[any_spec] * 10,
-        out_specs=(any_spec, pl.BlockSpec(memory_space=pltpu.VMEM)),
+        out_shape=(vmem(field, f32), vmem((members, SEC_DEV), f32)),
+        in_specs=[hbm_spec] * 10,
+        out_specs=(pl.BlockSpec(memory_space=pltpu.VMEM), pl.BlockSpec(memory_space=pltpu.VMEM)),
         scratch_shapes=[
             vmem(field, f32), vmem(field, f32), vmem(field, f32),
             vmem((8, 128), jnp.int32), vmem((members, K, 1, 128), f32), vmem((1, 128), jnp.int32),
             vmem((5,) + flat, jnp.bfloat16),
             *[vmem(flat, f32) for _ in range(8)],
             *[vmem(field, f32) for _ in range(4)],
-            vmem((PSTEPS, n_spec) + field, f32),
+            vmem((PSTEPS, side - 1, K) + lump, f32),
+            *[vmem((PSTEPS, K) + lump, f32) for _ in range(3)],
+            *[vmem((PSTEPS, side - 1, K) + lump, f32) for _ in range(2)],
             vmem((2 * PSTEPS, 2) + field, f32),
             vmem((n_space, 128), jnp.bfloat16),
             vmem((n_space, 1, 128), f32),
             vmem((n_sec, 1, 128), f32),
             pltpu.SemaphoreType.DMA((10,)),
-            pltpu.SemaphoreType.DMA((PSTEPS, n_spec)),
-            pltpu.SemaphoreType.DMA((PSTEPS, n_spec)),
+            pltpu.SemaphoreType.DMA((2, PSTEPS, side - 1, K)),
+            pltpu.SemaphoreType.DMA((2, PSTEPS, K)),
+            pltpu.SemaphoreType.DMA((2, PSTEPS, K)),
+            pltpu.SemaphoreType.DMA((2, PSTEPS, side - 1, K)),
             pltpu.SemaphoreType.DMA((2 * PSTEPS, 2)),
             pltpu.SemaphoreType.DMA((2 * PSTEPS, 2)),
             pltpu.SemaphoreType.DMA((2,)),
-            pltpu.SemaphoreType.DMA,
+            pltpu.SemaphoreType.REGULAR((5,)),
         ],
         compiler_params=pltpu.CompilerParams(
-            collective_id=0, has_side_effects=True, vmem_limit_bytes=40 * 1024 * 1024
+            collective_id=0, has_side_effects=True, vmem_limit_bytes=60 * 1024 * 1024
         ),
         name="adjoint",
     )(

time: 65.5 us -> 50.3 us (0.77)
  Pallas kernels: 56.2 us -> 48.3 us
  local copies, waits for them, and re-layouts: 8.32 us -> 1.22 us
    pallas_call x1, Pallas kernels: 56.2 us -> 48.3 us  [on_device(): pl.pallas_call(functools.partial(kernel, sizes), out_shape=(vmem(field, f...]
    unnamed x22 -> x2, local copies, waits for them, and re-layouts: 8.32 us -> 1.22 us
where the time goes in v2:
time: 50.3 us; the launch traced here: 50.2 us
  Pallas kernels  48.3 us (96%)
  local copies, waits for them, and re-layouts  1.22 us (2%)
  between operations  0.64 us (1%)
    pallas_call x1, Pallas kernels, on_device(): pl.pallas_call(functools.partial(kernel, sizes), out_shape=(vmem(field, f...  48.3 us
    unnamed x2, local copies, waits for them, and re-layouts  1.22 us

profile of v2, /device:TPU:1, one launch (start us, length us, event | category | flops | bytes accessed | tf_op | source)
XLA Modules:
  0.0 50.2 jit_solution(10169623424093023763)
XLA Ops:
  0.6 48.3 %adjoint.1 = (f32[4,5,8,128]{3,2,1,0:T(8,128)S(1)}, f32[4,8]{1,0:T(4,128)S(1)}) custom-call(f32[4,5,8,128]{3,2,1,0:T(8,128)} %bitcast.17, f32[4,5,8,128]{3,2,1,0:T(8,128)} %bitcast.18, bf16[800,128]{1,0:T(8,128)(2,1)} %bitcast.12, bf16[800,128]{1,0:T(8,128)(2,1)} %bitcast.13, bf16[800,128]{1,0:T(8,128)(2,1)} %bitcast.14, bf16[800,128]{1,0:T(8,128)(2,1)} %bitcast.15, ...), custom_call_target="tpu_custom_call" | custom-call | tf_op jit(solution)/shard_map/adjoint/pallas_call | solution.py:410
  49.0 0.6 %copy.15 = f32[4,5,1,8,128]{4,3,2,1,0:T(8,128)} copy(f32[4,5,1,8,128]{4,3,2,1,0:T(8,128)S(1)} %bitcast.11) | data formatting | bytes 163840
  49.6 0.6 %copy.16 = f32[4,8]{1,0:T(4,128)} copy(f32[4,8]{1,0:T(4,128)S(1)} %get-tuple-element.9) | data formatting | bytes 256

commit v3 on v2

--- a/solution.py
+++ b/solution.py
@@ -14,6 +14,7 @@
 GAIN = 0.25
 K = 5
 GATHER, SCATTER = (0, 1), (2, 3, 4)
+FAR, MATE = 0, 1
 MESH = pl.DeviceIdType.MESH
 
 
@@ -42,7 +43,7 @@
     a_ref, a1_ref, g_ref, col_ref, wall_ref, own_ref, raw,
     dm, pm, jsm, jnm, jcm, ps, pn, pc,
     rs, b_ref, u_ref, h_ref, ya_rx, xa_tx, xa_rx, xb_rx, yb_tx, yb_rx, halo_rx, dest_hot, sec_tx, sec_rx,
-    in_sem, ya_sem, xa_sem, xb_sem, yb_sem, halo_tx_sem, halo_rx_sem, sec_sem, known_sem,
+    in_sem, ya_sem, xa_sem, xb_sem, yb_sem, halo_sem, sec_sem, known_sem,
 ):
     members, n_inst, n_space, quads = sizes
     row = spectral_row(members * n_inst)
@@ -53,7 +54,10 @@
     high, why = inst // side, lax.rem(inst, side)
     y_peers = [(high * side + lax.rem(why + d, side), space) for d in range(1, side)]
     x_peer = (lax.rem(inst + side, n_inst), space)
-    halo_peers = [(inst, lax.rem(space + 1, n_space)), (inst, lax.rem(space + n_space - 1, n_space))]
+    even = lax.rem(space, 2) == 0
+    far = space + jnp.where(even, n_space - 1, 1)
+    halo_peers = {FAR: (inst, lax.rem(far, n_space)), MATE: (inst, space + jnp.where(even, 1, -1))}
+    far_there = jnp.logical_and(space > 0, space < n_space - 1)
     rings = n_space // quads
     zed, quad = space // quads, lax.rem(space, quads)
     sec_peers = []
@@ -63,7 +67,7 @@
                 sec_peers.append((inst, lax.rem(zed + dz, rings) * quads + lax.rem(quad + dq, quads)))
 
     barrier = pltpu.get_barrier_semaphore()
-    near = y_peers + [x_peer] + halo_peers
+    near = y_peers + [x_peer] + [halo_peers[FAR], halo_peers[MATE]]
     for peer in near:
         pl.semaphore_signal(barrier, inc=1, device_id=peer, device_id_type=MESH)
     loads = [
@@ -190,16 +194,18 @@
     def learn(turn):
         pl.semaphore_wait(known_sem.at[turn], 2)
 
-    def send_halo(slot, source):
-        halo = []
-        for side, peer in enumerate(halo_peers):
+    def send_halo(slot, source, part=None):
+        some = pl.ds(0, members) if part is None else pl.ds(part * (members // 2), members // 2)
+        copies = []
+        for which in (FAR, MATE):
             copy = pltpu.make_async_remote_copy(
-                src_ref=source, dst_ref=halo_rx.at[slot, side], send_sem=halo_tx_sem.at[slot, side],
-                recv_sem=halo_rx_sem.at[slot, side], device_id=peer, device_id_type=MESH,
+                src_ref=source.at[some], dst_ref=halo_rx.at[slot, which, some],
+                send_sem=halo_sem.at[0, slot, which, part or 0], recv_sem=halo_sem.at[1, slot, which, part or 0],
+                device_id=halo_peers[which], device_id_type=MESH,
             )
             copy.start()
-            halo.append(copy)
-        return halo
+            copies.append(copy)
+        return copies
 
     def block(ref, m, k, l):
         at = (m * K * K + k * K + l) * 8
@@ -218,9 +224,9 @@
         return pltpu.roll(v, 1, 1) - pltpu.roll(v, 127, 1)
 
     def span_diff(slot, m, l):
-        minus = jnp.where(space > 0, halo_rx[slot, 0, m, l], 0.0)
-        plus = jnp.where(space < n_space - 1, halo_rx[slot, 1, m, l], 0.0)
-        return minus - plus
+        far = jnp.where(far_there, halo_rx[slot, FAR, m, l], 0.0)
+        mate = halo_rx[slot, MATE, m, l]
+        return jnp.where(even, far - mate, mate - far)
 
     def fold():
         @pl.loop(0, members)
@@ -282,15 +288,6 @@
         tell(3 * step + 1)
         spectral_end(step, spec)
 
-        for m in range(members):
-            r = [rs[m, l] for l in range(K)]
-            for k in range(K):
-                total = block(pm, m, k, 0) * r[0]
-                for l in range(1, K):
-                    total = total + block(pm, m, k, l) * r[l]
-                b_ref[m, k] = total
-                u_ref[m, k] = jnp.where(colour == 0, total, 0.0)
-
         def cross_terms(m, source):
             v = [source[m, l] for l in range(K)]
             dn = [normal_diff(v[l]) for l in range(K)]
@@ -303,15 +300,31 @@
                 out.append(total)
             return v, out
 
-        @pl.loop(1, NCOL)
-        def _(value):
-            mine = colour == value
-            for m in range(members):
-                v, cross = cross_terms(m, u_ref)
-                for k in range(K):
-                    u_ref[m, k] = jnp.where(mine, b_ref[m, k] - cross[k], v[k])
-
-        halo_u = send_halo(2 * step + 1, u_ref)
+        def visit(mine, some, field):
+            for m in some:
+                v, cross = cross_terms(m, field)
+                for k in range(K):
+                    field[m, k] = jnp.where(mine, b_ref[m, k] - cross[k], v[k])
+
+        halves = [range(members // 2), range(members // 2, members)]
+
+        halo_u = []
+        for part, some in enumerate(halves):
+            for m in some:
+                r = [rs[m, l] for l in range(K)]
+                for k in range(K):
+                    total = block(pm, m, k, 0) * r[0]
+                    for l in range(1, K):
+                        total = total + block(pm, m, k, l) * r[l]
+                    b_ref[m, k] = total
+                    u_ref[m, k] = jnp.where(colour == 0, total, 0.0)
+
+            @pl.loop(1, NCOL)
+            def _(value, some=some):
+                visit(colour == value, some, u_ref)
+
+            halo_u.append(send_halo(2 * step + 1, u_ref, part))
+
         for m in range(members):
             _, cross = cross_terms(m, u_ref)
             for k in range(K):
@@ -319,26 +332,23 @@
         if step == 0:
             learn(1)
             tell(2)
-        for copy in halo_u:
-            copy.wait_recv()
-        for m in range(members):
-            ds = [span_diff(2 * step + 1, m, l) for l in range(K)]
-            for k in range(K):
-                total = b_ref[m, k]
-                for l in range(K):
-                    total = total - block(ps, m, k, l) * ds[l]
-                b_ref[m, k] = total
-                h_ref[m, k] = jnp.where(colour == NCOL - 1, total - rs[m, k], u_ref[m, k])
-
-        @pl.loop(1, NCOL)
-        def _(back):
-            mine = colour == NCOL - 1 - back
-            for m in range(members):
-                v, cross = cross_terms(m, h_ref)
-                for k in range(K):
-                    h_ref[m, k] = jnp.where(mine, b_ref[m, k] - cross[k], v[k])
-
-        sent = list(spec.values()) + halo_a + halo_u
+        for part, some in enumerate(halves):
+            for copy in halo_u[part]:
+                copy.wait_recv()
+            for m in some:
+                ds = [span_diff(2 * step + 1, m, l) for l in range(K)]
+                for k in range(K):
+                    total = b_ref[m, k]
+                    for l in range(K):
+                        total = total - block(ps, m, k, l) * ds[l]
+                    b_ref[m, k] = total
+                    h_ref[m, k] = jnp.where(colour == NCOL - 1, total - rs[m, k], u_ref[m, k])
+
+            @pl.loop(1, NCOL)
+            def _(back, some=some):
+                visit(colour == NCOL - 1 - back, some, h_ref)
+
+        sent = list(spec.values()) + halo_a + halo_u[0] + halo_u[1]
         if step < PSTEPS - 1:
             for m in range(members):
                 for k in range(K):
@@ -400,6 +410,15 @@
     every.wait_send()
 
 
+def finish(adj_ref, sens_ref, adj_out, sens_out, sem):
+    one = pltpu.make_async_copy(adj_ref, adj_out, sem.at[0])
+    two = pltpu.make_async_copy(sens_ref, sens_out, sem.at[1])
+    one.start()
+    two.start()
+    one.wait()
+    two.wait()
+
+
 def on_device(sizes, a, g, d, p, js, jn, jc, colour, wall, owner):
     members, n_inst, n_space, quads = sizes
     field = (members, K, 8, 128)
@@ -430,8 +449,7 @@
             pltpu.SemaphoreType.DMA((2, PSTEPS, K)),
             pltpu.SemaphoreType.DMA((2, PSTEPS, K)),
             pltpu.SemaphoreType.DMA((2, PSTEPS, side - 1, K)),
-            pltpu.SemaphoreType.DMA((2 * PSTEPS, 2)),
-            pltpu.SemaphoreType.DMA((2 * PSTEPS, 2)),
+            pltpu.SemaphoreType.DMA((2, 2 * PSTEPS, 2, 2)),
             pltpu.SemaphoreType.DMA((2,)),
             pltpu.SemaphoreType.REGULAR((5,)),
         ],
@@ -443,6 +461,15 @@
         a.reshape(field), g.reshape(field), *[x.reshape(flat) for x in (d, p, js, jn, jc)],
         colour.reshape(8, 128), wall, owner,
     )
+    adj, sens = pl.pallas_call(
+        finish,
+        out_shape=(jax.ShapeDtypeStruct(field, f32), jax.ShapeDtypeStruct((members, SEC_DEV), f32)),
+        in_specs=[pl.BlockSpec(memory_space=pltpu.VMEM)] * 2,
+        out_specs=(hbm_spec, hbm_spec),
+        scratch_shapes=[pltpu.SemaphoreType.DMA((2,))],
+        compiler_params=pltpu.CompilerParams(vmem_limit_bytes=1024 * 1024),
+        name="finish",
+    )(adj, sens)
     return adj.reshape(a.shape), sens
 
 

time: 50.3 us -> 49.6 us (0.986)
  local copies, waits for them, and re-layouts: 1.22 us -> 0 us
    unnamed x2 -> x0, local copies, waits for them, and re-layouts: 1.22 us -> none
    pallas_call x0 -> x1, Pallas kernels: none -> 0.66 us  [on_device(): pl.pallas_call(finish, out_shape=(jax.ShapeDtypeStruct(field, f32), jax.S...]
where the time goes in v3:
time: 49.6 us; the launch traced here: 49.4 us
  Pallas kernels  48.8 us (98%)
  between operations  0.64 us (1%)
    pallas_call x1, Pallas kernels, on_device(): pl.pallas_call(functools.partial(kernel, sizes), out_shape=(vmem(field, f...  48.1 us

profile of v3, /device:TPU:1, one launch (start us, length us, event | category | flops | bytes accessed | tf_op | source)
XLA Modules:
  0.0 49.4 jit_solution(18032966844600333792)
XLA Ops:
  0.6 48.1 %adjoint.1 = (f32[4,5,8,128]{3,2,1,0:T(8,128)S(1)}, f32[4,8]{1,0:T(4,128)S(1)}) custom-call(f32[4,5,8,128]{3,2,1,0:T(8,128)} %bitcast.16, f32[4,5,8,128]{3,2,1,0:T(8,128)} %bitcast.17, bf16[800,128]{1,0:T(8,128)(2,1)} %bitcast.11, bf16[800,128]{1,0:T(8,128)(2,1)} %bitcast.12, bf16[800,128]{1,0:T(8,128)(2,1)} %bitcast.13, bf16[800,128]{1,0:T(8,128)(2,1)} %bitcast.14, ...), custom_call_target="tpu_custom_call" | custom-call | tf_op jit(solution)/shard_map/adjoint/pallas_call | solution.py:429
  48.8 0.7 %finish.1 = (f32[4,5,8,128]{3,2,1,0:T(8,128)}, f32[4,8]{1,0:T(4,128)}) custom-call(f32[4,5,8,128]{3,2,1,0:T(8,128)S(1)} %get-tuple-element.6.adj_ref, f32[4,8]{1,0:T(4,128)S(1)} %get-tuple-element.7.sens_ref), custom_call_target="tpu_custom_call" | custom-call | tf_op jit(solution)/shard_map/finish/pallas_call | solution.py:464
